TPU v7x, 32 devices: a whole 2x2x4 slice. The times are simulated.
32 devices in a mesh: chan: 4 (over z), bin: 8 (over y, x, core).
Axes of the slice: x: 2, y: 2, z: 4, core: 2. Of those that a mesh axis runs over, the one named last changes fastest.
Arguments:
- spectra: bfloat16 [64, 2, 512, 1024], P('bin', None, None, 'chan')
- valid: int32 [8, 512], P('chan'), may hold values from 0 to 1, as said below
Outputs:
- stacked: bfloat16 [8, 5, 64, 2, 128, 128], P('chan', None, 'bin')
Inputs may be any that keep to these rules, and one draw needn't show every extreme that they name: `valid`: each entry is 0 or 1; in every draw exactly one channel block, drawn from the seed, has no usable segment at all.
All inputs are finite; a program needn't handle non-finite values.
Results may differ from a plain program's by a relative error of at most 0.0043.
Values may be sent and summed in bfloat16 or wider, within the bound.
A program may use at most 128 MiB of HBM per device.

v0:
```python
import jax
import jax.numpy as jnp
from jax import lax
from jax.sharding import PartitionSpec as P


def shifted(block, axis, distance):
    devices = range(lax.axis_size(axis))
    route = [((i - distance) % len(devices), i) for i in devices]
    return lax.ppermute(block, axis, route)


def cross_block(left, right, left_mask, right_mask):
    total = jnp.maximum(jnp.sum(left_mask * right_mask), 1.0)
    real_part = jnp.einsum(
        "fsa,fsb->fab", left[:, 0], right[:, 0], preferred_element_type=jnp.float32
    )
    real_part = real_part + jnp.einsum(
        "fsa,fsb->fab", left[:, 1], right[:, 1], preferred_element_type=jnp.float32
    )
    imag_part = jnp.einsum(
        "fsa,fsb->fab", left[:, 1], right[:, 0], preferred_element_type=jnp.float32
    )
    imag_part = imag_part - jnp.einsum(
        "fsa,fsb->fab", left[:, 0], right[:, 1], preferred_element_type=jnp.float32
    )
    return (jnp.stack([real_part, imag_part], axis=1) / total).astype(jnp.bfloat16)


def shards(spectra, valid):
    bin_devices = lax.axis_size("bin")
    chan_devices = lax.axis_size("chan")
    bins_here = spectra.shape[0]
    blocks_here = valid.shape[0]
    width = spectra.shape[3] // blocks_here
    block_count = blocks_here * chan_devices
    offsets = block_count // 2 + 1
    spectra32 = spectra.astype(jnp.float32)
    partial_value = jnp.sum(jnp.sqrt(spectra32[:, 0] ** 2 + spectra32[:, 1] ** 2), axis=0)
    amplitude = lax.psum(partial_value, "bin")
    keep = jnp.repeat(valid.astype(jnp.float32).T, width, axis=1)
    white = (spectra32 / (amplitude / (bins_here * bin_devices) + 1e-06) * keep).astype(
        jnp.bfloat16
    )
    own_mask = valid.astype(jnp.float32)
    results = [[None] * offsets for row_block in range(blocks_here)]

    def fill(blocks, masks, offset):
        masks_float = masks.astype(jnp.float32)
        for row_block in range(blocks_here):
            for col_block in range(blocks_here):
                lag = offset * blocks_here + col_block - row_block
                if 0 <= lag < offsets:
                    left = white[..., row_block * width : (row_block + 1) * width]
                    right = blocks[..., col_block * width : (col_block + 1) * width]
                    results[row_block][lag] = cross_block(
                        left, right, own_mask[row_block], masks_float[col_block]
                    )

    fill(white, valid, 0)
    farthest = (blocks_here - 1 + block_count // 2) // blocks_here
    moving = (white, valid)
    for offset in range(1, farthest + 1):
        moving = shifted((moving[0], moving[1]), "chan", -1)
        fill(moving[0], moving[1], offset)
    return jnp.stack([jnp.stack(row_list) for row_list in results])


def solution(mesh):
    return jax.shard_map(
        shards,
        mesh=mesh,
        in_specs=(P("bin", None, None, "chan"), P("chan", None)),
        out_specs=P("chan", None, "bin", None, None, None),
        check_vma=False,
    )
```

profile of v0, /device:TPU:0, one launch (start us, length us, event | category | flops | bytes accessed | tf_op | source)
XLA Modules:
  0.0 332.6 jit_solution(13590978603648099346)
XLA Ops:
  6.5 3.1 copy_convert_fusion
  9.6 2.3 fusion.2
  12.8 56.6 %all-reduce.2.cloned.1.call-done = f32[512,256]{1,0:T(8,128)} async-done(((f32[512,256]{1,0:T(8,128)}), f32[512,256]{1,0:T(8,128)}) %all-reduce.2.cloned.1.call-update) | async-done | bytes 524304 | tf_op jit(solution)/shard_map/psum | solution.py:40
  70.5 4.2 %multiply_convert_fusion = bf16[8,2,512,256]{3,2,0,1:T(8,128)(2,1)} fusion(f32[512,256]{1,0:T(8,128)S(1)} %bitcast.150, f32[512,256]{1,0:T(8,128)S(1)} %multiply_add_fusion, bf16[8,2,512,256]{3,2,1,0:T(8,128)(2,1)} %param.2), kind=kLoop, calls=%fused_computation | loop fusion | flops 8388608 | bytes 9437184 | tf_op jit(solution)/shard_map/convert_element_type | solution.py:42
  74.7 3.3 collective-permute-start
  78.5 88.7 %collective-permute-done.1 = s32[2,512]{1,0:T(2,128)S(1)} collective-permute-done((s32[2,512]{1,0:T(2,128)S(1)}, s32[2,512]{1,0:T(2,128)S(1)}, u32[]{:S(2)}, u32[]{:S(2)}) %collective-permute-start.1) | collective-permute-done | bytes 4128 | tf_op jit(solution)/shard_map/ppermute | solution.py:10
  167.2 4.3 %collective-permute-start.3 = (s32[2,512]{1,0:T(2,128)S(1)}, s32[2,512]{1,0:T(2,128)S(1)}, u32[]{:S(2)}, u32[]{:S(2)}) collective-permute-start(s32[2,512]{1,0:T(2,128)S(1)} %collective-permute-done.1), channel_id=1, source_target_pairs={{8,0},{16,8},{24,16},{0,24},{9,1},{17,9},{25,17},{1,25},{10,2},{18... | collective-permute-start | bytes 12296 | tf_op jit(solution)/shard_map/ppermute | solution.py:10
  179.7 2.1 fusion.60
  181.8 2.3 fusion.22
  184.1 2.0 fusion.59
  186.1 2.0 fusion.21
  188.2 2.1 fusion.63
  190.3 2.1 fusion.12
  192.5 2.0 fusion.62
  194.5 2.0 fusion.11
  196.7 2.0 fusion.61
  198.7 2.0 fusion.19
  200.7 2.0 fusion.58
  202.7 2.0 fusion.20
  205.0 2.0 fusion.36
  207.0 2.0 fusion.35
  209.0 4.3 %collective-permute-start.2 = (bf16[8,2,512,256]{3,2,0,1:T(8,128)(2,1)}, bf16[8,2,512,256]{3,2,0,1:T(8,128)(2,1)S(1)}, u32[]{:S(2)}, u32[]{:S(2)}) collective-permute-start(bf16[8,2,512,256]{3,2,0,1:T(8,128)(2,1)} %collective-permute-done), channel_id=1, source_target_pairs={{8,0},{16,8},{24,16},{0,24},{9,1},{17,9},{25,17},{1,25},{10,2},{18... | collective-permute-start | bytes 12582920 | tf_op jit(solution)/shard_map/ppermute | solution.py:10
  215.4 2.0 fusion.9
  217.6 2.0 fusion.40
  219.6 2.0 fusion.8
  223.6 2.0 fusion.7
  227.9 2.0 fusion.17
  234.1 2.0 fusion.41
  236.2 2.0 fusion.15
  238.2 2.0 fusion.42
  242.4 58.1 %collective-permute-done.2 = bf16[8,2,512,256]{3,2,0,1:T(8,128)(2,1)S(1)} collective-permute-done((bf16[8,2,512,256]{3,2,0,1:T(8,128)(2,1)}, bf16[8,2,512,256]{3,2,0,1:T(8,128)(2,1)S(1)}, u32[]{:S(2)}, u32[]{:S(2)}) %collective-permute-start.2) | collective-permute-done | bytes 4194336 | tf_op jit(solution)/shard_map/ppermute | solution.py:10
  322.3 3.5 %copy.45 = bf16[2,5,8,2,128,128]{5,4,3,2,1,0:T(8,128)(2,1)} copy(bf16[2,5,8,2,128,128]{5,4,2,3,1,0:T(8,128)(2,1)S(1)} %pad_maximum_fusion) | data formatting | bytes 10485760 | tf_op jit(solution)/shard_map/stack | solution.py:66
  (44 shorter events, 39.4 us)
Async XLA Ops:
  6.5 62.8 %all-reduce.2.cloned.1.call-start = ((), (), s32[]{:S(2)}) async-start(), calls=%async_computation | async-start | bytes 1048576 | tf_op jit(solution)/shard_map/psum | solution.py:40
  9.6 2.3 copy-start
  74.7 130.3 %collective-permute-start = (bf16[8,2,512,256]{3,2,0,1:T(8,128)(2,1)}, bf16[8,2,512,256]{3,2,0,1:T(8,128)(2,1)}, u32[]{:S(2)}, u32[]{:S(2)}) collective-permute-start(bf16[8,2,512,256]{3,2,0,1:T(8,128)(2,1)} %multiply_convert_fusion), channel_id=1, source_target_pairs={{8,0},{16,8},{24,16},{0,24},{9,1},{17,9},{25,17},{1,25},{10,2},{18... | collective-permute-start | bytes 12582920 | tf_op jit(solution)/shard_map/ppermute | solution.py:10
  77.9 89.3 %collective-permute-start.1 = (s32[2,512]{1,0:T(2,128)S(1)}, s32[2,512]{1,0:T(2,128)S(1)}, u32[]{:S(2)}, u32[]{:S(2)}) collective-permute-start(s32[2,512]{1,0:T(2,128)S(1)} %copy-done), channel_id=1, source_target_pairs={{8,0},{16,8},{24,16},{0,24},{9,1},{17,9},{25,17},{1,25},{10,2},{18... | collective-permute-start | bytes 12296 | tf_op jit(solution)/shard_map/ppermute | solution.py:10
  167.2 5.6 %collective-permute-start.3 = (s32[2,512]{1,0:T(2,128)S(1)}, s32[2,512]{1,0:T(2,128)S(1)}, u32[]{:S(2)}, u32[]{:S(2)}) collective-permute-start(s32[2,512]{1,0:T(2,128)S(1)} %collective-permute-done.1), channel_id=1, source_target_pairs={{8,0},{16,8},{24,16},{0,24},{9,1},{17,9},{25,17},{1,25},{10,2},{18... | collective-permute-start | bytes 12296 | tf_op jit(solution)/shard_map/ppermute | solution.py:10
  209.0 91.5 %collective-permute-start.2 = (bf16[8,2,512,256]{3,2,0,1:T(8,128)(2,1)}, bf16[8,2,512,256]{3,2,0,1:T(8,128)(2,1)S(1)}, u32[]{:S(2)}, u32[]{:S(2)}) collective-permute-start(bf16[8,2,512,256]{3,2,0,1:T(8,128)(2,1)} %collective-permute-done), channel_id=1, source_target_pairs={{8,0},{16,8},{24,16},{0,24},{9,1},{17,9},{25,17},{1,25},{10,2},{18... | collective-permute-start | bytes 12582920 | tf_op jit(solution)/shard_map/ppermute | solution.py:10
Sparse Core Ops, SparseCore 0:
  12.1 57.2 all-reduce.1
where the time goes:
time: 334 us; the launch traced here: 333 us
  waiting for transfers between devices  205 us (61%)
  matrix products  77.8 us (23%)
  between operations  19.9 us (6%)
  other arithmetic  13.6 us (4%)
  starting transfers between devices  12.4 us (4%)
  local copies, waits for them, and re-layouts  4.24 us (1%)
    ppermute x4, waiting for transfers between devices, shifted(): return lax.ppermute(block, axis, route)  148 us
    psum x1, waiting for transfers between devices, shards(): amplitude = lax.psum(partial_value, 'bin')  56.6 us
    dot_general x10, matrix products, cross_block(): jnp.einsum('fsa,fsb->fab', left[:, 1], right[:, 1], preferred_element_typ...  19.7 us
    dot_general x10, matrix products, cross_block(): jnp.einsum('fsa,fsb->fab', left[:, 0], right[:, 0], preferred_element_typ...  19.4 us
    dot_general x10, matrix products, cross_block(): jnp.einsum('fsa,fsb->fab', left[:, 1], right[:, 0], preferred_element_typ...  19.3 us
    dot_general x10, matrix products, cross_block(): jnp.einsum('fsa,fsb->fab', left[:, 0], right[:, 1], preferred_element_typ...  19.3 us
    ppermute x4, starting transfers between devices, shifted(): return lax.ppermute(block, axis, route)  12.4 us
  transfers between devices with their start and end apart: 5, of which 4 were waited for; matrix products, arithmetic and copies ran while one was open for 17% of the time, Pallas kernels for 0%

commit v1 on v0

--- a/solution.py
+++ b/solution.py
@@ -1,6 +1,10 @@
+import functools
+
 import jax
 import jax.numpy as jnp
 from jax import lax
+from jax.experimental import pallas as pl
+from jax.experimental.pallas import tpu as pltpu
 from jax.sharding import PartitionSpec as P
 
 
@@ -66,9 +70,431 @@
     return jnp.stack([jnp.stack(row_list) for row_list in results])
 
 
+def full_rows(row_block):
+    return (slice(0, 3), slice(2, 5)) if row_block == 0 else (slice(3, 7), slice(1, 5))
+
+
+def part_rows(row_block):
+    return (slice(2, 3), slice(4, 5)) if row_block == 0 else (slice(5, 7), slice(3, 5))
+
+
+def near_rows(row_block):
+    return (slice(0, 2), slice(2, 4)) if row_block == 0 else (slice(2, 4), slice(1, 3))
+
+
+def hub_kernel(
+    total_bins, x_ref, keep_ref, vrow_ref, out_ref, part, pieces, scale, masks, outer_raw, cross_raw,
+    white, stage, near_stage, raw_send, raw_recv, relay_send, cross_recv, part_send, part_recv,
+    scale_send, scale_recv, col_send, col_recv, mask_send, mask_recv,
+    stage_send, near_send, result_recv, near_recv, local_sem,
+):
+    z = lax.axis_index("chan")
+    b = lax.axis_index("bin")
+    peers = lax.axis_size("bin")
+    bins, _, seg, chans = x_ref.shape
+    width = chans // 2
+    half = bins // 2
+    rows = seg // peers
+    is_hub = (z == 1) | (z == 2)
+    is_outer = jnp.logical_not(is_hub)
+    outer_hub = jnp.where(z == 0, 1, 2)
+    other_hub = 3 - z
+    outer = jnp.where(z == 1, 0, 3)
+    other_outer = 3 - outer
+    cross_base = jnp.where(z == 1, half, 0)
+    relay_base = half - cross_base
+    first_base = jnp.where(z == 0, 0, half)
+
+    def peer(step):
+        return (z, lax.rem(b + step, peers))
+
+    def remote(src, dst, send, recv, device):
+        return pltpu.make_async_remote_copy(
+            src_ref=src, dst_ref=dst, send_sem=send, recv_sem=recv,
+            device_id=device, device_id_type=pl.DeviceIdType.MESH,
+        )
+
+    barrier = pltpu.get_barrier_semaphore()
+    for step in range(1, peers):
+        pl.semaphore_signal(barrier, inc=1, device_id=peer(step), device_id_type=pl.DeviceIdType.MESH)
+    for step in range(1, 4):
+        pl.semaphore_signal(
+            barrier, inc=1, device_id=(lax.rem(z + step, 4), b), device_id_type=pl.DeviceIdType.MESH
+        )
+    pl.semaphore_wait(barrier, peers - 1 + 3)
+
+    def outer_send(f):
+        return remote(x_ref.at[f], outer_raw.at[f], raw_send.at[f], raw_recv.at[f], (outer_hub, b))
+
+    def own_cross(n):
+        f = relay_base + n
+        return remote(
+            x_ref.at[f], cross_raw.at[0, n], raw_send.at[n], cross_recv.at[0, n], (other_hub, b)
+        )
+
+    def relay(n):
+        return remote(
+            outer_raw.at[relay_base + n], cross_raw.at[1, n], relay_send.at[n], cross_recv.at[1, n],
+            (other_hub, b),
+        )
+
+    @pl.when(is_outer)
+    def _():
+        for n in range(half):
+            outer_send(first_base + n).start()
+
+    @pl.when(is_hub)
+    def _():
+        for n in range(half):
+            own_cross(n).start()
+
+    def mask_copy(hub):
+        return remote(vrow_ref, masks.at[z], mask_send.at[hub - 1], mask_recv.at[z], (hub, b))
+
+    masks[z] = vrow_ref[...]
+    for hub in (1, 2):
+        @pl.when(z != hub)
+        def _():
+            mask_copy(hub).start()
+
+    def add_bins(i, carry):
+        at = pl.ds(pl.multiple_of(i * 16, 16), 16)
+        total = jnp.zeros((16, chans), jnp.float32)
+        for f in range(bins):
+            re = x_ref[f, 0, at, :].astype(jnp.float32)
+            im = x_ref[f, 1, at, :].astype(jnp.float32)
+            total = total + jnp.sqrt(re * re + im * im)
+        part[at, :] = total
+        return carry
+
+    lax.fori_loop(0, seg // 16, add_bins, 0)
+
+    def piece_rows(index):
+        return pl.ds(pl.multiple_of(index * rows, rows), rows)
+
+    def part_copy(step):
+        target = peer(step)
+        return remote(
+            part.at[piece_rows(target[1])], pieces.at[step - 1],
+            part_send.at[step - 1], part_recv.at[step - 1], target,
+        )
+
+    for step in range(1, peers):
+        part_copy(step).start()
+
+    @pl.when(is_outer)
+    def _():
+        for n in range(half):
+            outer_send(half - first_base + n).start()
+
+    for step in range(1, peers):
+        part_copy(step).wait_recv()
+    mine = piece_rows(b)
+    total = part[mine, :]
+    for step in range(1, peers):
+        total = total + pieces[step - 1]
+    scale[z, mine, :] = keep_ref[mine, :] / (total / total_bins + 1e-06)
+
+    def scale_copy(layer, step):
+        return remote(
+            scale.at[layer, mine], scale.at[layer, mine],
+            scale_send.at[layer, step - 1], scale_recv.at[layer, step - 1], peer(step),
+        )
+
+    def scale_arrival(layer, step):
+        source = piece_rows(lax.rem(b + peers - step, peers))
+        return remote(
+            scale.at[layer, source], scale.at[layer, source],
+            scale_send.at[layer, step - 1], scale_recv.at[layer, step - 1], peer(step),
+        )
+
+    def col_copy(hub):
+        return remote(
+            scale.at[z, mine], scale.at[z, mine], col_send.at[hub - 1], col_recv.at[z], (hub, b)
+        )
+
+    def col_arrival(layer):
+        return remote(
+            scale.at[layer, mine], scale.at[layer, mine], col_send.at[0], col_recv.at[layer],
+            (lax.rem(z + 1, 4), b),
+        )
+
+    def mask_arrival(layer):
+        return remote(
+            vrow_ref, masks.at[layer], mask_send.at[0], mask_recv.at[layer], (lax.rem(z + 1, 4), b)
+        )
+
+    for hub in (1, 2):
+        @pl.when(z != hub)
+        def _():
+            col_copy(hub).start()
+    for step in range(1, peers):
+        scale_copy(z, step).start()
+    for step in range(1, peers):
+        scale_arrival(z, step).wait_recv()
+
+    def whiten(src, slot, layer):
+        def chunk(i, carry):
+            at = pl.ds(pl.multiple_of(i * 64, 64), 64)
+            factor = scale[layer, at, :]
+            for p in range(2):
+                white[slot, p, at, :] = (src[p, at, :].astype(jnp.float32) * factor).astype(jnp.bfloat16)
+            return carry
+
+        lax.fori_loop(0, seg // 64, chunk, 0)
+
+    def dot(a, c):
+        return lax.dot_general(a, c, (((0,), (0,)), ((), ())), preferred_element_type=jnp.float32)
+
+    def cross(left, right, store, wanted):
+        lr, li = white[left, 0], white[left, 1]
+        rr, ri = white[right, 0], white[right, 1]
+        real = dot(lr, rr) + dot(li, ri)
+        imag = dot(li, rr) - dot(lr, ri)
+        for row, col in wanted:
+            weight = masks[left, row : row + 1, :] * masks[right, col : col + 1, :]
+            inverse = 1.0 / jnp.maximum(jnp.sum(weight, axis=1, keepdims=True), 1.0)
+            here = (slice(row * width, (row + 1) * width), slice(col * width, (col + 1) * width))
+            store(row, col, 0, (real[here] * inverse).astype(jnp.bfloat16))
+            store(row, col, 1, (imag[here] * inverse).astype(jnp.bfloat16))
+
+    def own_pairs(f):
+        def store(row, col, p, value):
+            out_ref[row, col - row, f, p] = value
+
+        whiten(x_ref.at[f], z, z)
+        cross(z, z, store, ((0, 0), (0, 1), (1, 1)))
+
+    everything = ((0, 0), (0, 1), (1, 0), (1, 1))
+
+    @pl.when(is_outer)
+    def _():
+        def body(f, carry):
+            own_pairs(f)
+            return carry
+
+        lax.fori_loop(0, bins, body, 0)
+
+    def near_copy(n, row):
+        src, dst = near_rows(row)
+        return remote(
+            near_stage.at[n, src], out_ref.at[row, dst, n], near_send.at[n, row], near_recv.at[n, row],
+            (0, b),
+        )
+
+    def near_local(n, row):
+        src, dst = near_rows(row)
+        return pltpu.make_async_copy(
+            near_stage.at[n, src], out_ref.at[row, dst, relay_base + n], near_send.at[n, row]
+        )
+
+    def full_copy(n, target, row, f):
+        src, dst = full_rows(row)
+        return remote(
+            stage.at[n, target, src], out_ref.at[row, dst, f], stage_send.at[n, target, row],
+            result_recv.at[f, row], (target, b),
+        )
+
+    def part_result(n, target, row, f):
+        src, dst = part_rows(row)
+        return remote(
+            stage.at[n, target, src], out_ref.at[row, dst, f], stage_send.at[n, target, row],
+            result_recv.at[f, row], (target, b),
+        )
+
+    def local_copy(n, row):
+        src, dst = full_rows(row)
+        return pltpu.make_async_copy(
+            stage.at[n, z, src], out_ref.at[row, dst, cross_base + n], local_sem.at[n, row]
+        )
+
+    lower = 2 * (z - 1)
+
+    @pl.when(is_hub)
+    def _():
+        for distance in range(1, 4):
+            layer = lax.rem(z + distance, 4)
+            col_arrival(layer).wait_recv()
+            for step in range(1, peers):
+                scale_copy(layer, step).start()
+
+        for distance in range(1, 4):
+            layer = lax.rem(z + distance, 4)
+            mask_arrival(layer).wait_recv()
+            for step in range(1, peers):
+                scale_arrival(layer, step).wait_recv()
+
+        def near(n, carry):
+            f = relay_base + n
+            remote(x_ref.at[f], outer_raw.at[f], raw_send.at[f], raw_recv.at[f], (outer, b)).wait_recv()
+            relay(n).start()
+            own_pairs(f)
+            whiten(outer_raw.at[f], outer, outer)
+
+            def store(row, col, p, value):
+                near_stage[n, 2 * row + col, p] = value
+
+            cross(lower, lower + 1, store, everything)
+
+            @pl.when(z == 1)
+            def _():
+                for row in range(2):
+                    near_copy(n, row).start()
+
+            @pl.when(z == 2)
+            def _():
+                for row in range(2):
+                    near_local(n, row).start()
+
+            return carry
+
+        lax.fori_loop(0, half, near, 0)
+
+        def far(n, carry):
+            f = cross_base + n
+            own_pairs(f)
+            remote(x_ref.at[f], outer_raw.at[f], raw_send.at[f], raw_recv.at[f], (outer, b)).wait_recv()
+            whiten(outer_raw.at[f], outer, outer)
+            own_cross(n).wait_recv()
+            whiten(cross_raw.at[0, n], other_hub, other_hub)
+            relay(n).wait_recv()
+            whiten(cross_raw.at[1, n], other_outer, other_outer)
+
+            def one_row(d, inner):
+                def store(row, col, p, value):
+                    stage[n, d, 3 * row + col, p] = value
+
+                def store_far(row, col, p, value):
+                    stage[n, d, 2 + 3 * row + col, p] = value
+
+                cross(d, lax.rem(d + 1, 4), store, everything)
+                cross(d, lax.rem(d + 2, 4), store_far, ((0, 0), (1, 0), (1, 1)))
+                return inner
+
+            lax.fori_loop(0, 4, one_row, 0)
+            for row in range(2):
+                part_result(n, 4 - 2 * z, row, f).start()
+                full_copy(n, 3, row, f).start()
+                full_copy(n, z - 1, row, f).start()
+                local_copy(n, row).start()
+            return carry
+
+        lax.fori_loop(0, half, far, 0)
+
+    @pl.when(z == 0)
+    def _():
+        for n in range(half):
+            for row in range(2):
+                near_copy(n, row).wait_recv()
+                part_result(n, 0, row, n).wait_recv()
+                full_copy(n, 0, row, half + n).wait_recv()
+
+    @pl.when(z == 1)
+    def _():
+        for n in range(half):
+            for row in range(2):
+                full_copy(n, 1, row, n).wait_recv()
+
+    @pl.when(z == 2)
+    def _():
+        for n in range(half):
+            for row in range(2):
+                part_result(n, 2, row, half + n).wait_recv()
+
+    @pl.when(z == 3)
+    def _():
+        for f in range(bins):
+            for row in range(2):
+                full_copy(f % half, 3, row, f).wait_recv()
+
+    @pl.when(is_outer)
+    def _():
+        for f in range(bins):
+            outer_send(f).wait_send()
+
+    @pl.when(is_hub)
+    def _():
+        for n in range(half):
+            own_cross(n).wait_send()
+            relay(n).wait_send()
+            for row in range(2):
+                f = cross_base + n
+                part_result(n, 4 - 2 * z, row, f).wait_send()
+                full_copy(n, 3, row, f).wait_send()
+                full_copy(n, z - 1, row, f).wait_send()
+                local_copy(n, row).wait()
+        for distance in range(1, 4):
+            for step in range(1, peers):
+                scale_copy(lax.rem(z + distance, 4), step).wait_send()
+
+    @pl.when(z == 1)
+    def _():
+        for n in range(half):
+            for row in range(2):
+                near_copy(n, row).wait_send()
+
+    @pl.when(z == 2)
+    def _():
+        for n in range(half):
+            for row in range(2):
+                near_local(n, row).wait()
+
+    for hub in (1, 2):
+        @pl.when(z != hub)
+        def _():
+            mask_copy(hub).wait_send()
+            col_copy(hub).wait_send()
+    for step in range(1, peers):
+        part_copy(step).wait_send()
+        scale_copy(z, step).wait_send()
+
+
+def hub_shards(spectra, valid):
+    peers = lax.axis_size("bin")
+    bins, _, seg, chans = spectra.shape
+    width = chans // 2
+    half = bins // 2
+    valid_float = valid.astype(jnp.float32)
+    keep = jnp.repeat(valid_float.T, width, axis=1)
+    rows = jnp.tile(valid_float, (4, 1))
+    dma = pltpu.SemaphoreType.DMA
+    vmem = pl.BlockSpec(memory_space=pltpu.VMEM)
+    block = (2, seg, chans)
+    result = (2, width, width)
+    return pl.pallas_call(
+        functools.partial(hub_kernel, bins * peers),
+        out_shape=jax.ShapeDtypeStruct((2, 5, bins) + result, jnp.bfloat16),
+        in_specs=[vmem] * 3,
+        out_specs=vmem,
+        scratch_shapes=[
+            pltpu.VMEM((seg, chans), jnp.float32),
+            pltpu.VMEM((peers - 1, seg // peers, chans), jnp.float32),
+            pltpu.VMEM((4, seg, chans), jnp.float32),
+            pltpu.VMEM((4, 8, seg), jnp.float32),
+            pltpu.VMEM((bins,) + block, jnp.bfloat16),
+            pltpu.VMEM((2, half) + block, jnp.bfloat16),
+            pltpu.VMEM((4,) + block, jnp.bfloat16),
+            pltpu.VMEM((half, 4, 7) + result, jnp.bfloat16),
+            pltpu.VMEM((half, 4) + result, jnp.bfloat16),
+            dma((bins,)), dma((bins,)), dma((half,)), dma((2, half)),
+            dma((peers - 1,)), dma((peers - 1,)),
+            dma((4, peers - 1)), dma((4, peers - 1)), dma((2,)), dma((4,)), dma((2,)), dma((4,)),
+            dma((half, 4, 2)), dma((half, 2)), dma((bins, 2)), dma((half, 2)), dma((half, 2)),
+        ],
+        compiler_params=pltpu.CompilerParams(
+            collective_id=0, has_side_effects=True, vmem_limit_bytes=56 * 2**20
+        ),
+        cost_estimate=pl.CostEstimate(
+            flops=40 * bins * 2 * seg * width * width * 8, bytes_accessed=2 * spectra.size * 4,
+            transcendentals=spectra.size // 2,
+        ),
+    )(spectra, keep, rows)
+
+
 def solution(mesh):
+    in_line = mesh.shape["chan"] == 4
     return jax.shard_map(
-        shards,
+        hub_shards if in_line else shards,
         mesh=mesh,
         in_specs=(P("bin", None, None, "chan"), P("chan", None)),
         out_specs=P("chan", None, "bin", None, None, None),

time: 334 us -> 237 us (0.71)
  Pallas kernels: 0 us -> 223 us
  waiting for transfers between devices: 205 us -> 0 us
  matrix products: 77.8 us -> 0 us
  between operations: 19.9 us -> 0.02 us
  other arithmetic: 13.6 us -> 0.69 us
  starting transfers between devices: 12.4 us -> 0 us
  local copies, waits for them, and re-layouts: 4.24 us -> 9.16 us
    pallas_call x0 -> x1, Pallas kernels: none -> 223 us  [hub_shards(): pl.pallas_call(functools.partial(hub_kernel, bins * peers), out_shape=jax...]
    ppermute x4 -> x0, waiting for transfers between devices: 148 us -> none  [shifted(): return lax.ppermute(block, axis, route)]
    dot_general x40 -> x0, matrix products: 77.8 us -> none  [the longest x10 19.7 us: cross_block(): jnp.einsum('fsa,fsb->fab', left[:, 1], right[:, 1], preferred_element_typ...]
    psum x1 -> x0, waiting for transfers between devices: 56.6 us -> none  [shards(): amplitude = lax.psum(partial_value, 'bin')]
    ppermute x4 -> x0, starting transfers between devices: 12.4 us -> none  [shifted(): return lax.ppermute(block, axis, route)]
    unnamed x3 -> x2, local copies, waits for them, and re-layouts: 0.04 us -> 7.8 us
    convert_element_type x5 -> x1, other arithmetic: 7.31 us -> 0.69 us  [hub_shards(): valid_float = valid.astype(jnp.float32)]
  transfers between devices with their start and end apart: 5 -> 0, of which waited for: 4 -> 0; matrix products, arithmetic and copies ran while one was open for 17% -> 0% of each run, Pallas kernels for 0% -> 0%
where the time goes in v1:
time: 237 us; the launch traced here: 233 us
  Pallas kernels  223 us (94%)
  local copies, waits for them, and re-layouts  9.16 us (4%)
    pallas_call x1, Pallas kernels, hub_shards(): pl.pallas_call(functools.partial(hub_kernel, bins * peers), out_shape=jax...  223 us
    unnamed x2, local copies, waits for them, and re-layouts  7.8 us

profile of v1, /device:TPU:0, one launch (start us, length us, event | category | flops | bytes accessed | tf_op | source)
XLA Modules:
  0.0 232.9 jit_solution(3352423781739118644)
XLA Ops:
  0.0 0.7 fusion
  0.7 0.6 tile.10.vrow_ref
  1.3 0.1 copy.3
  1.5 0.6 broadcast_in_dim.3
  2.1 0.8 copy.6
  2.9 223.1 %shard_map.28 = bf16[2,5,8,2,128,128]{5,4,3,2,1,0:T(8,128)(2,1)} custom-call(bf16[8,2,512,256]{3,2,1,0:T(8,128)(2,1)} %x_ref.1, f32[512,256]{1,0:T(8,128)} %bitcast.7, f32[8,512]{1,0:T(8,128)} %tile.10.vrow_ref), custom_call_target="tpu_custom_call" | custom-call | flops 42949672960 | bytes 16777216 | tf_op jit(solution)/shard_map/pallas_call | solution.py:464
  226.0 7.0 %copy.8 = bf16[2,5,8,2,128,128]{5,4,3,2,1,0:T(8,128)(2,1)} copy(bf16[2,5,8,2,128,128]{5,4,3,2,1,0:T(8,128)(2,1)} %shard_map.28) | data formatting | bytes 10485760
  (1 shorter events, 0.0 us)

commit v2 on v1

--- a/solution.py
+++ b/solution.py
@@ -126,6 +126,9 @@
     def outer_send(f):
         return remote(x_ref.at[f], outer_raw.at[f], raw_send.at[f], raw_recv.at[f], (outer_hub, b))
 
+    def outer_arrival(f):
+        return remote(x_ref.at[f], outer_raw.at[f], raw_send.at[f], raw_recv.at[f], (outer, b))
+
     def own_cross(n):
         f = relay_base + n
         return remote(
@@ -140,12 +143,12 @@
 
     @pl.when(is_outer)
     def _():
-        for n in range(half):
+        for n in range(half - 1):
             outer_send(first_base + n).start()
 
     @pl.when(is_hub)
     def _():
-        for n in range(half):
+        for n in range(half // 2):
             own_cross(n).start()
 
     def mask_copy(hub):
@@ -182,10 +185,10 @@
     for step in range(1, peers):
         part_copy(step).start()
 
-    @pl.when(is_outer)
-    def _():
-        for n in range(half):
-            outer_send(half - first_base + n).start()
+    @pl.when(is_hub)
+    def _():
+        for n in range(half // 2, half - 1):
+            own_cross(n).start()
 
     for step in range(1, peers):
         part_copy(step).wait_recv()
@@ -230,6 +233,20 @@
             col_copy(hub).start()
     for step in range(1, peers):
         scale_copy(z, step).start()
+
+    @pl.when(is_outer)
+    def _():
+        outer_send(first_base + half - 1).start()
+        for n in range(half):
+            outer_send(half - first_base + n).start()
+
+    @pl.when(is_hub)
+    def _():
+        own_cross(half - 1).start()
+        for n in range(half):
+            outer_arrival(relay_base + n).wait_recv()
+            relay(n).start()
+
     for step in range(1, peers):
         scale_arrival(z, step).wait_recv()
 
@@ -312,22 +329,20 @@
 
     @pl.when(is_hub)
     def _():
-        for distance in range(1, 4):
-            layer = lax.rem(z + distance, 4)
+        for layer in (outer, other_hub, other_outer):
             col_arrival(layer).wait_recv()
             for step in range(1, peers):
                 scale_copy(layer, step).start()
 
-        for distance in range(1, 4):
-            layer = lax.rem(z + distance, 4)
+        def layer_arrival(layer):
             mask_arrival(layer).wait_recv()
             for step in range(1, peers):
                 scale_arrival(layer, step).wait_recv()
 
+        layer_arrival(outer)
+
         def near(n, carry):
             f = relay_base + n
-            remote(x_ref.at[f], outer_raw.at[f], raw_send.at[f], raw_recv.at[f], (outer, b)).wait_recv()
-            relay(n).start()
             own_pairs(f)
             whiten(outer_raw.at[f], outer, outer)
 
@@ -349,11 +364,13 @@
             return carry
 
         lax.fori_loop(0, half, near, 0)
+        layer_arrival(other_hub)
+        layer_arrival(other_outer)
 
         def far(n, carry):
             f = cross_base + n
             own_pairs(f)
-            remote(x_ref.at[f], outer_raw.at[f], raw_send.at[f], raw_recv.at[f], (outer, b)).wait_recv()
+            outer_arrival(f).wait_recv()
             whiten(outer_raw.at[f], outer, outer)
             own_cross(n).wait_recv()
             whiten(cross_raw.at[0, n], other_hub, other_hub)

time: 237 us -> 172 us (0.73)
  the two profiles are of different devices: /device:TPU:0 before, /device:TPU:25 now
where the time goes in v2:
time: 172 us
  Pallas kernels  162 us (94%)
  local copies, waits for them, and re-layouts  9.16 us (5%)
    pallas_call x1, Pallas kernels, hub_shards(): pl.pallas_call(functools.partial(hub_kernel, bins * peers), out_shape=jax...  162 us
    unnamed x2, local copies, waits for them, and re-layouts  7.8 us

profile of v2, /device:TPU:25, one launch (start us, length us, event | category | flops | bytes accessed | tf_op | source)
XLA Modules:
  0.0 171.7 jit_solution(16812977887040628153)
XLA Ops:
  0.0 0.7 fusion
  0.7 0.6 tile.10.vrow_ref
  1.3 0.1 copy.3
  1.5 0.6 broadcast_in_dim.3
  2.1 0.8 copy.6
  2.9 161.9 %shard_map.28 = bf16[2,5,8,2,128,128]{5,4,3,2,1,0:T(8,128)(2,1)} custom-call(bf16[8,2,512,256]{3,2,1,0:T(8,128)(2,1)} %x_ref.1, f32[512,256]{1,0:T(8,128)} %bitcast.7, f32[8,512]{1,0:T(8,128)} %tile.10.vrow_ref), custom_call_target="tpu_custom_call" | custom-call | flops 42949672960 | bytes 16777216 | tf_op jit(solution)/shard_map/pallas_call | solution.py:481
  164.8 7.0 %copy.8 = bf16[2,5,8,2,128,128]{5,4,3,2,1,0:T(8,128)(2,1)} copy(bf16[2,5,8,2,128,128]{5,4,3,2,1,0:T(8,128)(2,1)} %shard_map.28) | data formatting | bytes 10485760
  (1 shorter events, 0.0 us)

commit v3 on v2

--- a/solution.py
+++ b/solution.py
@@ -377,22 +377,35 @@
             relay(n).wait_recv()
             whiten(cross_raw.at[1, n], other_outer, other_outer)
 
-            def one_row(d, inner):
+            def near_row(d):
                 def store(row, col, p, value):
                     stage[n, d, 3 * row + col, p] = value
 
-                def store_far(row, col, p, value):
+                cross(d, lax.rem(d + 1, 4), store, everything)
+
+            def far_row(d):
+                def store(row, col, p, value):
                     stage[n, d, 2 + 3 * row + col, p] = value
 
-                cross(d, lax.rem(d + 1, 4), store, everything)
-                cross(d, lax.rem(d + 2, 4), store_far, ((0, 0), (1, 0), (1, 1)))
+                cross(d, lax.rem(d + 2, 4), store, ((0, 0), (1, 0), (1, 1)))
+
+            near_row(5 - 2 * z)
+            far_row(5 - 2 * z)
+            for row in range(2):
+                full_copy(n, 5 - 2 * z, row, f).start()
+            far_row(4 - 2 * z)
+            for row in range(2):
+                part_result(n, 4 - 2 * z, row, f).start()
+
+            def one_row(j, inner):
+                d = jnp.where(j == 0, 3 * z - 3, z)
+                near_row(d)
+                far_row(d)
                 return inner
 
-            lax.fori_loop(0, 4, one_row, 0)
-            for row in range(2):
-                part_result(n, 4 - 2 * z, row, f).start()
-                full_copy(n, 3, row, f).start()
-                full_copy(n, z - 1, row, f).start()
+            lax.fori_loop(0, 2, one_row, 0)
+            for row in range(2):
+                full_copy(n, 3 * z - 3, row, f).start()
                 local_copy(n, row).start()
             return carry
 

time: 172 us -> 174 us (1.012)
  the two profiles are of different devices: /device:TPU:25 before, /device:TPU:0 now
where the time goes in v3:
time: 174 us; the launch traced here: 173 us
  Pallas kernels  163 us (94%)
  local copies, waits for them, and re-layouts  9.16 us (5%)
    pallas_call x1, Pallas kernels, hub_shards(): pl.pallas_call(functools.partial(hub_kernel, bins * peers), out_shape=jax...  163 us
    unnamed x2, local copies, waits for them, and re-layouts  7.8 us

profile of v3, /device:TPU:0, one launch (start us, length us, event | category | flops | bytes accessed | tf_op | source)
XLA Modules:
  0.0 173.4 jit_solution(3411951062754345221)
XLA Ops:
  0.0 0.7 fusion
  0.7 0.6 tile.10.vrow_ref
  1.3 0.1 copy.3
  1.5 0.6 broadcast_in_dim.3
  2.1 0.8 copy.6
  2.9 163.5 %shard_map.28 = bf16[2,5,8,2,128,128]{5,4,3,2,1,0:T(8,128)(2,1)} custom-call(bf16[8,2,512,256]{3,2,1,0:T(8,128)(2,1)} %x_ref.1, f32[512,256]{1,0:T(8,128)} %bitcast.7, f32[8,512]{1,0:T(8,128)} %tile.10.vrow_ref), custom_call_target="tpu_custom_call" | custom-call | flops 42949672960 | bytes 16777216 | tf_op jit(solution)/shard_map/pallas_call | solution.py:494
  166.4 7.0 %copy.8 = bf16[2,5,8,2,128,128]{5,4,3,2,1,0:T(8,128)(2,1)} copy(bf16[2,5,8,2,128,128]{5,4,3,2,1,0:T(8,128)(2,1)} %shard_map.28) | data formatting | bytes 10485760
  (1 shorter events, 0.0 us)
